TPU v7x, 128 devices: a whole 4x4x4 slice. The times are simulated.
128 devices in a mesh: wide: 32 (over z, x_hi, y), narrow: 4 (over x_lo, core).
Axes of the slice: x: 4 (x_hi: 2, x_lo: 2; x = x_hi * 2 + x_lo), y: 4, z: 4, core: 2. Of those that a mesh axis runs over, the one named last changes fastest.
Arguments:
- amplitudes: float32 [2, 4, 1024, 1024], P(None, None, 'wide', 'narrow'), may hold values from -2 to 2
- cycle_amps: bfloat16 [2, 64, 1024, 1024], P(None, None, 'wide', 'narrow'), may hold values from -6 to 6
- cycle_ints: bfloat16 [64, 1024, 4, 1024], P(None, 'wide'), may hold values from -0.25 to 0.25
- ladder_ints: bfloat16 [64, 4, 1024, 1024], P(None, None, 'wide', 'narrow'), may hold values from -0.01171875 to 0.01171875
- integrals: float32 [2, 4, 1024, 1024], P(None, None, 'wide', 'narrow'), may hold values from -13 to 13
- history: float32 [4, 2, 4, 1024, 1024], P(None, None, None, 'wide', 'narrow'), may hold values from -22 to 22
- vir_energy: float32 [1024], replicated, may hold values from 0.5 to 3
- occ_first: float32 [2], replicated, may hold values from -1.5 to -0.3
- occ_second: float32 [4], replicated, may hold values from -1.2 to -0.2
Outputs:
- updated: float32 [2, 4, 1024, 1024], P(None, None, 'wide', 'narrow')
- residual: float32 [2, 4, 1024, 1024], P(None, None, 'wide', 'narrow')
- energy: float32 [1], replicated
- intersections: float32 [5], replicated
All inputs are finite; a program needn't handle non-finite values.
Results may differ from a plain program's by a relative error of at most 0.0003.
Values sent between devices are 32-bit elements; how exact they have to be, the bound alone decides.
A program may use at most 128 MiB of HBM per device.

v0:
```python
import jax
import jax.numpy as jnp
from jax import lax
from jax.sharding import PartitionSpec as P

NI = 2
NJ = 4
AWD = 2
BWD = 1


def place_block(own_block, local_rows, local_cols):
    row_take = own_block.shape[2]
    col_take = own_block.shape[3]
    return jnp.pad(
        own_block, ((0, 0), (0, 0), (0, local_rows - row_take), (0, local_cols - col_take))
    )


def shards(
    amplitudes,
    cycle_amps,
    cycle_ints,
    ladder_ints,
    integrals,
    history,
    vir_energy,
    occ_first,
    occ_second,
):
    wide_count = lax.axis_size("wide")
    narrow_count = lax.axis_size("narrow")
    wide_block = lax.axis_index("wide")
    narrow_block = lax.axis_index("narrow")
    local_rows = amplitudes.shape[2]
    local_cols = amplitudes.shape[3]
    partial_cycle = jnp.einsum(
        "ikca,kcjb->ijba", cycle_amps, cycle_ints, preferred_element_type=jnp.float32
    )
    rounded = amplitudes.astype(jnp.bfloat16).reshape(NI * NJ, local_rows * local_cols)
    ladder_rows_all = ladder_ints.shape[0]
    ladder_cols_all = ladder_ints.shape[1]
    flat_ints = ladder_ints.reshape(ladder_rows_all * ladder_cols_all, local_rows * local_cols)
    ladder_part = lax.dot_general(
        rounded, flat_ints, (((1,), (1,)), ((), ())), preferred_element_type=jnp.float32
    )
    ladder_part = ladder_part.reshape(NI, NJ, ladder_rows_all, ladder_cols_all)
    cycle_sum = lax.psum_scatter(partial_cycle, "wide", scatter_dimension=2, tiled=True)
    ladder_sum = lax.psum(ladder_part, ("wide", "narrow"))
    own_block = lax.dynamic_slice(
        ladder_sum, (0, 0, wide_block * AWD, narrow_block * BWD), (NI, NJ, AWD, BWD)
    )
    combined = cycle_sum + place_block(own_block, local_rows, local_cols)
    energy_rows = lax.dynamic_slice_in_dim(vir_energy, wide_block * local_rows, local_rows)
    energy_cols = lax.dynamic_slice_in_dim(vir_energy, narrow_block * local_cols, local_cols)
    denominator = (
        energy_rows[None, None, :, None]
        + energy_cols[None, None, None, :]
        - occ_first[:, None, None, None]
        - occ_second[None, :, None, None]
    )
    residual = integrals + combined - denominator * amplitudes
    updated = amplitudes + residual / denominator
    history_part = jnp.einsum("hijab,ijab->h", history, residual, precision=lax.Precision.HIGHEST)
    local_intersections = jnp.concatenate([history_part, jnp.sum(residual * residual)[None]])
    local_energy = jnp.sum(updated * integrals)[None]
    energy_sum, intersection_sum = lax.psum((local_energy, local_intersections), ("wide", "narrow"))
    cell_count = float(NI * NJ * local_rows * wide_count * local_cols * narrow_count)
    return (updated, residual, energy_sum / cell_count, intersection_sum / cell_count)


def solution(mesh):
    return jax.shard_map(
        shards,
        mesh=mesh,
        in_specs=(
            P(None, None, "wide", "narrow"),
            P(None, None, "wide", "narrow"),
            P(None, "wide", None, None),
            P(None, None, "wide", "narrow"),
            P(None, None, "wide", "narrow"),
            P(None, None, None, "wide", "narrow"),
            P(),
            P(),
            P(),
        ),
        out_specs=(P(None, None, "wide", "narrow"), P(None, None, "wide", "narrow"), P(), P()),
        check_vma=False,
    )
```

profile of v0, /device:TPU:1, one launch (start us, length us, event | category | flops | bytes accessed | tf_op | source)
XLA Modules:
  0.0 312.9 jit_solution(315918577524979840)
XLA Ops:
  7.2 0.0 copy-start
  7.2 0.0 reduce-scatter.2.cloned.1.call-start
  7.2 1.5 copy-done
  8.8 15.5 %fusion.5 = f32[2,4,1024,256]{3,2,0,1:T(8,128)} fusion(bf16[64,32,4,1024,1]{3,2,1,0,4:T(4,128)(2,1)} %bitcast.26, bf16[2,64,32,256]{3,2,1,0:T(8,128)(2,1)S(1)} %copy-done), kind=kOutput, calls=%fused_computation.5 | convolution fusion | flops 8589934592 | bytes 27262976 | tf_op jit(solution)/shard_map/ikca,kcjb->ijba/dot_general | solution.py:37
  24.3 0.0 copy-start.1
  24.3 0.0 reduce-scatter.2.cloned.1.call-update
  24.3 0.0 copy-start.4
  24.3 0.0 copy-start.2
  24.4 0.0 copy-start.3
  24.4 0.8 dynamic_slice.11
  25.2 0.8 dynamic_slice.10
  25.9 0.0 copy-done.1
  26.0 4.7 %fusion.9 = f32[2,4,64,4]{2,1,3,0:T(4,128)S(1)} fusion(bf16[64,4,32,256]{3,2,1,0:T(8,128)(2,1)} %param.12, bf16[2,4,32,256,1]{3,2,1,0,4:T(8,128)(2,1)S(1)} %convert_bitcast_fusion), kind=kOutput, calls=%fused_computation.7 | convolution fusion | flops 33554432 | bytes 4333568 | tf_op jit(solution)/shard_map/dot_general | solution.py:44
  30.7 0.2 copy.17
  30.9 76.2 %psum.21 = f32[2,4,64,4]{3,2,0,1:T(8,128)S(1)} all-reduce(f32[2,4,64,4]{3,2,0,1:T(8,128)S(1)} %copy.17), channel_id=1, replica_groups=mesh['wide'=32,'narrow'=4] {'wide','narrow'}, use_global_device_ids=true, to_apply=%region_1.0 | all-reduce | flops 2048 | bytes 16384 | tf_op jit(solution)/shard_map/psum | solution.py:49
  107.0 0.1 constant_dynamic-slice_fusion
  107.1 0.1 broadcast_add_fusion
  107.2 0.0 copy-done.4
  107.2 0.1 broadcast_subtract_fusion
  107.3 100.2 %reduce-scatter.2.cloned.1.call-done = f32[2,4,32,256]{3,2,0,1:T(8,128)} async-done(((f32[2,4,1024,256]{3,2,0,1:T(8,128)}), f32[2,4,32,256]{3,2,0,1:T(8,128)}) %reduce-scatter.2.cloned.1.call-update) | async-done | bytes 262160 | tf_op jit(solution)/shard_map/reduce_scatter | solution.py:48
  207.5 0.0 copy-done.2
  207.5 0.0 copy-done.3
  207.5 1.7 multiply_reduce_fusion
  209.2 0.8 multiply_reduce_fusion.1
  210.0 0.7 copy.23
  210.7 0.7 copy.22
  211.4 6.1 %convolution_bitcast_fusion = f32[4]{0:T(128)S(1)} fusion(f32[4,2,4,32,256]{4,3,2,1,0:T(8,128)} %param.14, f32[2,4,32,256,1]{3,2,0,1,4:T(8,128)S(1)} %bitcast.25), kind=kOutput, calls=%fused_computation.8 | convolution fusion | flops 3145728 | bytes 1310736 | tf_op jit(solution)/shard_map/hijab,ijab->h/dot_general | solution.py:64
  217.5 0.7 pad_maximum_fusion
  218.2 85.6 %all-reduce.1 = (f32[1]{0:T(128)}, f32[5]{0:T(128)S(1)}) all-reduce(f32[1]{0:T(128)} %bitcast.8, f32[5]{0:T(128)S(1)} %pad_maximum_fusion), channel_id=1, replica_groups=mesh['wide'=32,'narrow'=4] {'wide','narrow'}, use_global_device_ids=true, to_apply=%region_3.4 | all-reduce | flops 6 | bytes 48 | tf_op jit(solution)/shard_map/psum | solution.py:67
  303.8 0.5 broadcast_multiply_fusion
  (1 shorter events, 0.0 us)
Async XLA Ops:
  7.2 1.6 copy-start
  7.2 200.4 %reduce-scatter.2.cloned.1.call-start = ((), (), s32[]{:S(2)}) async-start(), calls=%async_computation.1 | async-start | bytes 8650752 | tf_op jit(solution)/shard_map/reduce_scatter | solution.py:48
  24.3 1.6 copy-start.1
  24.3 82.9 %copy-start.4 = (f32[2]{0:T(128)S(1)}, f32[2]{0:T(128)}, u32[]{:S(2)}) copy-start(f32[2]{0:T(128)} %param.16) | copy-start | bytes 28
  24.3 183.2 %copy-start.2 = (f32[2,4,32,256]{3,2,1,0:T(8,128)S(1)}, f32[2,4,32,256]{3,2,1,0:T(8,128)}, u32[]{:S(2)}) copy-start(f32[2,4,32,256]{3,2,1,0:T(8,128)} %param.13) | copy-start | bytes 786436
  24.4 183.2 %copy-start.3 = (f32[4]{0:T(128)S(1)}, f32[4]{0:T(128)}, u32[]{:S(2)}) copy-start(f32[4]{0:T(128)} %param.17) | copy-start | bytes 52
Sparse Core Ops, SparseCore 0:
  24.4 183.0 reduce-scatter.1
where the time goes:
time: 313 us
  blocking collectives  162 us (52%)
  waiting for transfers between devices  100 us (32%)
  matrix products  26.3 us (8%)
  between operations  15.9 us (5%)
  local copies, waits for them, and re-layouts  4.82 us (2%)
  other arithmetic  3.86 us (1%)
    reduce_scatter x1, waiting for transfers between devices, shards(): lax.psum_scatter(partial_cycle, 'wide', scatter_dimension=2, tiled=True)  100 us
    psum x1, blocking collectives, shards(): lax.psum((local_energy, local_intersections), ('wide', 'narrow'))  85.6 us
    psum x1, blocking collectives, shards(): ladder_sum = lax.psum(ladder_part, ('wide', 'narrow'))  76.2 us
    dot_general x1, matrix products, shards(): jnp.einsum('ikca,kcjb->ijba', cycle_amps, cycle_ints, preferred_element_t...  15.5 us
  transfers between devices with their start and end apart: 1, of which 1 were waited for; matrix products, arithmetic and copies ran while one was open for 2% of the time, Pallas kernels for 0%

commit v1 on v0

v1 whole, which is shorter than its diff:
```python
import jax
import jax.numpy as jnp
from jax import lax
from jax.experimental import pallas as pl
from jax.experimental.pallas import tpu as pltpu
from jax.sharding import PartitionSpec as P

NI = 2
NJ = 4
DEPTH = 2048
MESH = pl.DeviceIdType.MESH
CHUNKS = (2, 1, 3, 0)
F32 = jnp.float32


def kernel(
    amp_hbm, u_hbm, m_hbm, lad_hbm, itg_hbm, his_hbm, vir_hbm, of_ref, os_ref,
    upd_hbm, res_hbm, ene_ref, int_ref,
    mbuf, ubuf, wbuf, part, r1, rx, r3,
    lbuf, lgrp, lsum, lrecv_n, lrecv_z, lrecv_x, lrecv_y,
    amp, itg, his, vir, upd, res, sc_x, sc_y, sc_z,
    lsem, s1, q1, sx, qx, s3, q3, sl, ql, ss, qs,
):
    wide = lax.axis_index("wide")
    narrow = lax.axis_index("narrow")
    z = wide // 8
    xh = lax.rem(wide // 4, 2)
    y = lax.rem(wide, 4)
    xl = narrow // 2
    core = lax.rem(narrow, 2)
    xpos = xh * 2 + xl

    def at(z_, y_, x_, core_):
        return {
            "wide": lax.rem(z_, 4) * 8 + lax.rem(x_, 4) // 2 * 4 + lax.rem(y_, 4),
            "narrow": lax.rem(x_, 2) * 2 + lax.rem(core_, 2),
        }

    def along(axis, delta):
        if axis == "z":
            return at(z + delta, y, xpos, core)
        if axis == "y":
            return at(z, y + delta, xpos, core)
        return at(z, y, xpos + delta, core)

    barrier = pltpu.get_barrier_semaphore()
    greeted = [along("z", d) for d in (1, 2, 3)] + [along("y", d) for d in (1, 2, 3)]
    greeted += [at(z, y, xpos + d // 2, core + d % 2) for d in range(1, 8)]
    for device in greeted:
        pl.semaphore_signal(barrier, inc=1, device_id=device, device_id_type=MESH)

    loads = {}

    def load(name, src, dst, n):
        loads[name] = pltpu.make_async_copy(src, dst, lsem.at[n])
        loads[name].start()

    def columns(c):
        zc = lax.rem(z + CHUNKS[c], 4)
        return pl.ds(pl.multiple_of(zc * 256, 256), 256)

    load("u", u_hbm, ubuf, 0)
    for c in range(4):
        load(("m", c), m_hbm.at[:, :, columns(c)], mbuf.at[c], 1 + c)
    load("amp", amp_hbm, amp, 5)
    load("lad", lad_hbm, lbuf, 6)
    load("itg", itg_hbm, itg, 7)
    load("his", his_hbm, his, 8)
    load("vir", vir_hbm, vir, 9)

    sends = []
    posted = {}

    def send(key, src, dst, ssem, rsem, device):
        copy = pltpu.make_async_remote_copy(
            src_ref=src, dst_ref=dst, send_sem=ssem, recv_sem=rsem, device_id=device, device_id_type=MESH
        )
        copy.start()
        sends.append(copy)
        posted[key] = copy

    ring_axis = ("z", "y")
    ring_pos = (z, y)
    chunk_pos = (y, z)

    def places(cls, ring_offset, c):
        ring = lax.rem(ring_pos[cls] + ring_offset, 4)
        chunk = lax.rem(chunk_pos[cls] + CHUNKS[c], 4)
        return (ring, chunk) if cls == 0 else (chunk, ring)

    def whole(cls, i, ring_offset, c):
        zp, yp = places(cls, ring_offset, c)
        return part.at[pl.ds(2 * cls, 2), i, zp, :, yp]

    def own_x(cls, i, c):
        zp, yp = places(cls, 0, c)
        return part.at[pl.ds(2 * cls, 2), i, zp, xh, yp]

    def ring_send(cls, kind, c, i, ring_offset, step):
        send(("r", cls, kind, c), whole(cls, i, ring_offset, c), r1.at[cls, kind, c],
             s1.at[cls, kind, c], q1.at[cls, kind, c], along(ring_axis[cls], step))

    def m1(cls, c):
        ring_send(cls, 0, c, 0, 2, 1)
        ring_send(cls, 1, c, 1, 2, 3)

    def m2_up(cls, c):
        ring_send(cls, 2, c, 1, 1, 1)

    def m2_down(cls, c):
        ring_send(cls, 3, c, 0, 3, 3)

    def m3_up(cls, c):
        posted["r", cls, 0, c].wait_recv()
        ref = whole(cls, 0, 1, c)
        ref[...] += r1[cls, 0, c]
        ring_send(cls, 4, c, 0, 1, 1)

    def m3_down(cls, c):
        posted["r", cls, 1, c].wait_recv()
        ref = whole(cls, 1, 3, c)
        ref[...] += r1[cls, 1, c]
        ring_send(cls, 5, c, 1, 3, 3)

    def ring_end(cls, c):
        for kind in (2, 3, 4, 5):
            posted["r", cls, kind, c].wait_recv()
        first = whole(cls, 0, 0, c)
        first[...] += r1[cls, 4, c] + r1[cls, 3, c]
        second = whole(cls, 1, 0, c)
        second[...] += r1[cls, 2, c] + r1[cls, 5, c]
        zp, yp = places(cls, 0, c)
        send(("x", cls, c), part.at[pl.ds(2 * cls, 2), :, zp, 1 - xh, yp], rx.at[cls, c],
             sx.at[cls, c], qx.at[cls, c], along("x", 2))

    def pair_end(cls, c):
        posted["x", cls, c].wait_recv()
        zp, yp = places(cls, 0, c)
        ref = part.at[pl.ds(2 * cls, 2), :, zp, xh, yp]
        ref[...] += rx[cls, c]

    def late_send(cls, kind, c, i, step):
        send(("l", cls, kind), own_x(cls, i, c), r3.at[cls, kind], s3.at[cls, kind], q3.at[cls, kind],
             along(ring_axis[1 - cls], step))

    def late0(cls):
        pair_end(cls, 0)
        late_send(cls, 0, 0, 0, 1)
        late_send(cls, 1, 0, 1, 3)

    def late1(cls):
        pair_end(cls, 1)
        late_send(cls, 2, 1, 1, 1)
        posted["l", cls, 0].wait_recv()
        ref = own_x(cls, 0, 1)
        ref[...] += r3[cls, 0]
        late_send(cls, 4, 1, 0, 1)

    def late2(cls):
        pair_end(cls, 2)
        late_send(cls, 3, 2, 0, 3)
        posted["l", cls, 1].wait_recv()
        ref = own_x(cls, 1, 2)
        ref[...] += r3[cls, 1]
        late_send(cls, 5, 2, 1, 3)

    def late3(cls):
        pair_end(cls, 3)
        for kind in (2, 3, 4, 5):
            posted["l", cls, kind].wait_recv()
        first = own_x(cls, 0, 3)
        first[...] += r3[cls, 4] + r3[cls, 3]
        second = own_x(cls, 1, 3)
        second[...] += r3[cls, 2] + r3[cls, 5]

    def relayout(c):
        loads["m", c].wait()

        def body(t, carry):
            k0 = pl.multiple_of(t * 64, 64)
            wbuf[:, pl.ds(k0, 64), :] = jnp.swapaxes(mbuf[c, pl.ds(k0, 64)], 0, 1)
            return carry

        lax.fori_loop(0, DEPTH // 64, body, 0)

    def product(c, cls):
        zp = lax.rem(z + CHUNKS[c], 4)

        def body(t, carry):
            j = 2 * cls + t
            for i in range(NI):
                got = lax.dot_general(wbuf[j], ubuf[i], (((0,), (0,)), ((), ())), preferred_element_type=F32)
                part[j, i, zp] = got.reshape(2, 4, 32, 256)
            return carry

        lax.fori_loop(0, 2, body, 0)

    def ladder_product():
        loads["amp"].wait()
        loads["lad"].wait()
        rounded = amp[...].reshape(256, 256).astype(jnp.bfloat16)
        row = lax.broadcasted_iota(jnp.int32, (32, 256), 0)
        lane = lax.broadcasted_iota(jnp.int32, (32, 256), 1)
        same = jnp.where(lax.rem(lane, 32) == row, 1.0, 0.0).astype(F32)

        def body(t, carry):
            s = lax.rem(t, 4)
            r0 = pl.multiple_of(t // 4 * 8, 8)
            ints = lbuf[pl.ds(r0, 8), s].reshape(256, 256)
            full = lax.dot_general(ints, rounded, (((1,), (1,)), ((), ())), preferred_element_type=F32)
            lgrp[s, pl.ds(r0, 8), :] = jnp.sum(full.reshape(8, 32, 256) * same[None], axis=1)
            return carry

        lax.fori_loop(0, 32, body, 0)
        group = lax.broadcasted_iota(jnp.int32, (256, 128), 0) // 32
        slot = lax.broadcasted_iota(jnp.int32, (256, 128), 1)
        pick = jnp.where(group == slot, 1.0, 0.0).astype(F32)
        lsum[...] = jnp.dot(
            lgrp[...].reshape(256, 256), pick, precision=lax.Precision.HIGHEST, preferred_element_type=F32
        ).reshape(4, 4, 2, 8, 128)
        for d in range(1, 4):
            peer_narrow = lax.rem(narrow + d, 4)
            send(("n", d), lsum.at[peer_narrow], lrecv_n.at[d - 1], sl.at[d - 1], ql.at[d - 1],
                 {"wide": wide, "narrow": peer_narrow})

    def ladder_z():
        for d in range(1, 4):
            posted["n", d].wait_recv()
        lsum[narrow] = lsum[narrow] + lrecv_n[0] + lrecv_n[1] + lrecv_n[2]
        for d in range(1, 4):
            send(("lz", d), lsum.at[narrow, lax.rem(z + d, 4)], lrecv_z.at[d - 1], sl.at[2 + d], ql.at[2 + d],
                 along("z", d))

    def ladder_x():
        for d in range(1, 4):
            posted["lz", d].wait_recv()
        lsum[narrow, z] = lsum[narrow, z] + lrecv_z[0] + lrecv_z[1] + lrecv_z[2]
        send("lx", lsum.at[narrow, z, 1 - xh], lrecv_x, sl.at[6], ql.at[6], along("x", 2))

    def ladder_y():
        posted["lx"].wait_recv()
        lsum[narrow, z, xh] = lsum[narrow, z, xh] + lrecv_x[...]
        for d in range(1, 4):
            send(("ly", d), lsum.at[narrow, z, xh], lrecv_y.at[d - 1], sl.at[6 + d], ql.at[6 + d], along("y", d))

    def ladder_end():
        for d in range(1, 4):
            posted["ly", d].wait_recv()
        total = lsum[narrow, z, xh] + lrecv_y[0] + lrecv_y[1] + lrecv_y[2]
        row = lax.broadcasted_iota(jnp.int32, (8, 128), 0)
        return [jnp.sum(jnp.where(row == 2 * y + e, total, 0.0), axis=0, keepdims=True) for e in range(2)]

    def fold(x):
        eight = jnp.sum(x.reshape(4, 8, 256), axis=0)
        return eight[:, :128] + eight[:, 128:]

    def tail(cls, ladder_rows, sums):
        row = lax.broadcasted_iota(jnp.int32, (32, 256), 0)
        lane = lax.broadcasted_iota(jnp.int32, (32, 256), 1)
        lane1 = lax.broadcasted_iota(jnp.int32, (1, 128), 1)
        lanes = lax.broadcasted_iota(jnp.int32, (32, 128), 1)
        rows = lax.broadcasted_iota(jnp.int32, (32, 128), 0)
        block = vir[:, pl.ds(pl.multiple_of(wide // 4 * 128, 128), 128)]
        down = jnp.sum(jnp.where(lanes == lax.rem(wide, 4) * 32 + rows, block, 0.0), axis=1, keepdims=True)
        across = vir[:, pl.ds(pl.multiple_of(narrow * 256, 256), 256)]
        for j in (2 * cls, 2 * cls + 1):
            for i in range(NI):
                ij = i * NJ + j
                placed = jnp.zeros((32, 256), F32)
                for e in range(2):
                    one = jnp.sum(jnp.where(lane1 == ij, ladder_rows[e], 0.0), axis=1, keepdims=True)
                    placed = jnp.where((row == e) & (lane == 0), one, placed)
                denominator = down + across - of_ref[i] - os_ref[j]
                a = amp[i, j]
                v = itg[i, j]
                r = v + part[j, i, z, xh, y] + placed - denominator * a
                new = a + r / denominator
                res[i, j] = r
                upd[i, j] = new
                terms = [new * v] + [his[h, i, j] * r for h in range(4)] + [r * r]
                sums = [s + fold(t) for s, t in zip(sums, terms)]
        return sums

    loads["u"].wait()
    relayout(0)
    product(0, 0)
    pl.semaphore_wait(barrier, len(greeted))
    m1(0, 0)
    m1(0, 1)
    product(0, 1)
    m1(1, 0)
    m2_up(1, 0)
    m2_down(1, 0)
    m1(0, 2)
    m1(0, 3)

    relayout(1)
    m3_up(1, 0)
    m3_down(1, 0)
    product(1, 0)
    m2_up(0, 0)
    m3_up(0, 0)
    product(1, 1)
    m1(1, 1)
    m2_up(1, 1)
    m2_down(1, 1)

    relayout(2)
    ring_end(1, 0)
    m3_up(1, 1)
    m3_down(1, 1)
    product(2, 0)
    m2_down(0, 0)
    m3_down(0, 0)
    m2_up(0, 1)
    m2_down(0, 1)
    m3_up(0, 1)
    m3_down(0, 1)
    product(2, 1)
    m1(1, 2)
    m2_up(1, 2)
    m2_down(1, 2)

    relayout(3)
    late0(1)
    m3_up(1, 2)
    m3_down(1, 2)
    product(3, 0)
    ring_end(1, 1)
    product(3, 1)
    m1(1, 3)
    m2_up(1, 3)
    m2_down(1, 3)
    ring_end(0, 0)

    def both(c):
        m2_up(0, c)
        m2_down(0, c)
        m3_up(0, c)
        m3_down(0, c)

    both(2)
    ladder_product()
    late1(1)
    late0(0)
    ring_end(0, 1)
    both(3)
    m3_up(1, 3)
    m3_down(1, 3)
    ladder_z()
    ring_end(1, 2)
    ladder_x()
    late1(0)
    ring_end(0, 2)
    late2(1)
    ladder_y()
    for name in ("itg", "his", "vir"):
        loads[name].wait()
    rows = ladder_end()
    late2(0)
    ring_end(1, 3)
    ring_end(0, 3)
    late3(1)
    sums = tail(1, rows, [jnp.zeros((8, 128), F32)] * 6)
    late3(0)
    sums = tail(0, rows, sums)

    stores = [pltpu.make_async_copy(upd, upd_hbm, lsem.at[10]), pltpu.make_async_copy(res, res_hbm, lsem.at[11])]
    for store in stores:
        store.start()

    eight = lax.broadcasted_iota(jnp.int32, (8, 128), 0)
    tile = jnp.zeros((8, 128), F32)
    for n, s in enumerate(sums):
        tile = jnp.where(eight == n, jnp.sum(s, axis=0, keepdims=True), tile)

    def everyone(buf, own, members, devices, first):
        count = len(devices) + 1
        buf[own] = tile
        for n, (device, member) in enumerate(zip(devices, members)):
            send(("s", first + n), buf.at[own], buf.at[own], ss.at[first + n], qs.at[first + n], device)
        for n, member in enumerate(members):
            pltpu.make_async_remote_copy(
                src_ref=buf.at[own], dst_ref=buf.at[member], send_sem=ss.at[first + n], recv_sem=qs.at[first + n],
                device_id=devices[n], device_id_type=MESH,
            ).wait_recv()
        total = buf[0]
        for n in range(1, count):
            total = total + buf[n]
        return total

    def chip_member(d):
        return lax.rem(xpos + 4 - d // 2, 4) * 2 + lax.rem(core + 2 - d % 2, 2)

    tile = everyone(sc_x, xpos * 2 + core, [chip_member(d) for d in range(1, 8)],
                    [at(z, y, xpos + d // 2, core + d % 2) for d in range(1, 8)], 0)
    tile = everyone(sc_y, y, [lax.rem(y + 4 - d, 4) for d in (1, 2, 3)], [along("y", d) for d in (1, 2, 3)], 7)
    tile = everyone(sc_z, z, [lax.rem(z + 4 - d, 4) for d in (1, 2, 3)], [along("z", d) for d in (1, 2, 3)], 10)

    scale = 1.0 / 8388608.0
    tile = jnp.sum(tile, axis=1, keepdims=True) * scale
    ene_ref[0] = tile[0, 0]
    for n in range(5):
        int_ref[n] = tile[n + 1, 0]
    for store in stores:
        store.wait()
    for copy in sends:
        copy.wait_send()


def shards(amplitudes, cycle_amps, cycle_ints, ladder_ints, integrals, history, vir_energy, occ_first, occ_second):
    anywhere = pl.BlockSpec(memory_space=pl.ANY)
    smem = pl.BlockSpec(memory_space=pltpu.SMEM)
    bf16 = jnp.bfloat16
    dma = pltpu.SemaphoreType.DMA
    block = jax.ShapeDtypeStruct((NI, NJ, 32, 256), F32)
    return pl.pallas_call(
        kernel,
        out_shape=(block, block, jax.ShapeDtypeStruct((1,), F32), jax.ShapeDtypeStruct((5,), F32)),
        in_specs=[anywhere] * 7 + [smem] * 2,
        out_specs=(anywhere, anywhere, smem, smem),
        scratch_shapes=[
            pltpu.VMEM((4, DEPTH, 4, 256), bf16),
            pltpu.VMEM((NI, DEPTH, 256), bf16),
            pltpu.VMEM((4, DEPTH, 256), bf16),
            pltpu.VMEM((NJ, NI, 4, 2, 4, 32, 256), F32),
            pltpu.VMEM((2, 6, 4, 2, 2, 32, 256), F32),
            pltpu.VMEM((2, 4, 2, 2, 32, 256), F32),
            pltpu.VMEM((2, 6, 2, 32, 256), F32),
            pltpu.VMEM((64, 4, 32, 256), bf16),
            pltpu.VMEM((4, 64, 256), F32),
            pltpu.VMEM((4, 4, 2, 8, 128), F32),
            pltpu.VMEM((3, 4, 2, 8, 128), F32),
            pltpu.VMEM((3, 2, 8, 128), F32),
            pltpu.VMEM((8, 128), F32),
            pltpu.VMEM((3, 8, 128), F32),
            pltpu.VMEM((NI, NJ, 32, 256), F32),
            pltpu.VMEM((NI, NJ, 32, 256), F32),
            pltpu.VMEM((4, NI, NJ, 32, 256), F32),
            pltpu.VMEM((1, 1024), F32),
            pltpu.VMEM((NI, NJ, 32, 256), F32),
            pltpu.VMEM((NI, NJ, 32, 256), F32),
            pltpu.VMEM((8, 8, 128), F32),
            pltpu.VMEM((4, 8, 128), F32),
            pltpu.VMEM((4, 8, 128), F32),
            dma((12,)),
            dma((2, 6, 4)), dma((2, 6, 4)),
            dma((2, 4)), dma((2, 4)),
            dma((2, 6)), dma((2, 6)),
            dma((10,)), dma((10,)),
            dma((13,)), dma((13,)),
        ],
        compiler_params=pltpu.CompilerParams(
            collective_id=0, has_side_effects=True, vmem_limit_bytes=58 * 2**20
        ),
        cost_estimate=pl.CostEstimate(flops=9 * 10**9, bytes_accessed=27 * 10**6, transcendentals=0),
        name="window",
    )(
        amplitudes,
        cycle_amps.reshape(NI, DEPTH, 256),
        cycle_ints.reshape(DEPTH, 4, 1024),
        ladder_ints,
        integrals,
        history,
        vir_energy.reshape(1, 1024),
        occ_first,
        occ_second,
    )


def solution(mesh):
    spread = P(None, None, "wide", "narrow")
    return jax.shard_map(
        shards,
        mesh=mesh,
        in_specs=(
            spread,
            spread,
            P(None, "wide", None, None),
            spread,
            spread,
            P(None, None, None, "wide", "narrow"),
            P(),
            P(),
            P(),
        ),
        out_specs=(spread, spread, P(), P()),
        check_vma=False,
    )
```

time: 313 us -> 88.1 us (0.28)
  blocking collectives: 162 us -> 0 us
  waiting for transfers between devices: 100 us -> 0 us
  Pallas kernels: 0 us -> 80.3 us
  matrix products: 26.3 us -> 0 us
  between operations: 15.9 us -> 2.34 us
  other arithmetic: 3.86 us -> 0 us
    psum x2 -> x0, blocking collectives: 162 us -> none  [the longest x1 85.6 us: shards(): lax.psum((local_energy, local_intersections), ('wide', 'narrow'))]
    reduce_scatter x1 -> x0, waiting for transfers between devices: 100 us -> none  [shards(): lax.psum_scatter(partial_cycle, 'wide', scatter_dimension=2, tiled=True)]
    pallas_call x0 -> x1, Pallas kernels: none -> 80.3 us  [shards(): pl.pallas_call(kernel, out_shape=(block, block, jax.ShapeDtypeStruct((1,)...]
    dot_general x3 -> x0, matrix products: 26.3 us -> none  [the longest x1 15.5 us: shards(): jnp.einsum('ikca,kcjb->ijba', cycle_amps, cycle_ints, preferred_element_t...]
  transfers between devices with their start and end apart: 1 -> 0, of which waited for: 1 -> 0; matrix products, arithmetic and copies ran while one was open for 2% -> 0% of each run, Pallas kernels for 0% -> 0%
where the time goes in v1:
time: 88.1 us; the launch traced here: 87.1 us
  Pallas kernels  80.3 us (91%)
  local copies, waits for them, and re-layouts  4.52 us (5%)
  between operations  2.34 us (3%)
    pallas_call x1, Pallas kernels, shards(): pl.pallas_call(kernel, out_shape=(block, block, jax.ShapeDtypeStruct((1,)...  80.3 us
    unnamed x3, local copies, waits for them, and re-layouts  4.52 us

profile of v1, /device:TPU:1, one launch (start us, length us, event | category | flops | bytes accessed | tf_op | source)
XLA Modules:
  0.0 87.1 jit_solution(9340500743913170217)
XLA Ops:
  0.6 80.3 %window.1 = (f32[2,4,32,256]{3,2,1,0:T(8,128)}, f32[2,4,32,256]{3,2,1,0:T(8,128)}, f32[1]{0:T(128)}, f32[5]{0:T(128)}) custom-call(f32[2,4,32,256]{3,2,1,0:T(8,128)} %amp_hbm.1, bf16[2,2048,256]{2,1,0:T(8,128)(2,1)} %bitcast.4, bf16[2048,4,1024]{2,1,0:T(4,128)(2,1)} %bitcast.3, bf16[64,4,32,256]{3,2,1,0:T(8,128)(2,1)} %lad_hbm.1, f32[2,4,32,256]{3,2,1,0:T(8,128)} %itg_hbm.1, ...), custom_call_target="tpu_custom_call" | custom-call | flops 8999999488 | bytes 27000000 | tf_op jit(solution)/shard_map/window/pallas_call | solution.py:417
  80.9 1.7 %copy.17 = f32[2,4,32,256]{3,2,1,0:T(8,128)} copy(f32[2,4,32,256]{3,2,1,0:T(8,128)} %get-tuple-element.8) | data formatting | bytes 524288
  82.6 1.7 %copy.18 = f32[2,4,32,256]{3,2,1,0:T(8,128)} copy(f32[2,4,32,256]{3,2,1,0:T(8,128)} %get-tuple-element.9) | data formatting | bytes 524288
  84.8 1.2 %copy.20 = f32[5]{0:T(128)} copy(f32[5]{0:T(128)} %get-tuple-element.11) | data formatting | bytes 40

commit v2 on v1

v2 whole, which is shorter than its diff:
```python
import jax
import jax.numpy as jnp
from jax import lax
from jax.experimental import pallas as pl
from jax.experimental.pallas import tpu as pltpu
from jax.sharding import PartitionSpec as P

NI = 2
NJ = 4
DEPTH = 2048
MESH = pl.DeviceIdType.MESH
CHUNKS = (2, 1, 3, 0)
F32 = jnp.float32


def kernel(
    amp_hbm, u_hbm, m_hbm, lad_hbm, itg_hbm, his_hbm, vir_hbm, of_hbm, os_hbm,
    upd, res, ene_ref, int_ref,
    mbuf, ubuf, wbuf, part, r0, r1, rx, rf, r3,
    lbuf, lgrp, lsum, lrecv_a, lplane, lrecv_b,
    amp, itg, his, vir, of_ref, os_ref, sums_a, sums_b,
    lsem, s0, q0, s1, q1, sx, qx, s3, q3, sl, ql, ss, qs,
):
    wide = lax.axis_index("wide")
    narrow = lax.axis_index("narrow")
    z = wide // 8
    xh = lax.rem(wide // 4, 2)
    y = lax.rem(wide, 4)
    xl = narrow // 2
    core = lax.rem(narrow, 2)
    xpos = xh * 2 + xl

    def at(z_, y_, x_, core_):
        return {
            "wide": lax.rem(z_, 4) * 8 + lax.rem(x_, 4) // 2 * 4 + lax.rem(y_, 4),
            "narrow": lax.rem(x_, 2) * 2 + lax.rem(core_, 2),
        }

    def along(axis, delta):
        if axis == "z":
            return at(z + delta, y, xpos, core)
        if axis == "y":
            return at(z, y + delta, xpos, core)
        return at(z, y, xpos + delta, core)

    barrier = pltpu.get_barrier_semaphore()
    plane = [at(z + d // 4, y + d % 4, xpos, core) for d in range(1, 16)]
    row_of_chips = [at(z, y, xpos + d // 2, core + d % 2) for d in range(1, 8)]
    for device in plane + row_of_chips:
        pl.semaphore_signal(barrier, inc=1, device_id=device, device_id_type=MESH)

    loads = {}

    def load(name, src, dst, n):
        loads[name] = pltpu.make_async_copy(src, dst, lsem.at[n])
        loads[name].start()

    def columns(c, x0, width):
        zc = lax.rem(z + CHUNKS[c], 4)
        return pl.ds(pl.multiple_of(zc * 256 + x0, 128), width)

    for q in range(4):
        rows_q = pl.ds(q * (DEPTH // 4), DEPTH // 4)
        load(("q", q), m_hbm.at[rows_q, :, columns(0, 0, 256)], mbuf.at[0, rows_q], 12 + q)
    load("u", u_hbm, ubuf, 0)

    def load_rest():
        for c in (3, 1, 2):
            load(("m", c), m_hbm.at[:, :, columns(c, 0, 256)], mbuf.at[c], 1 + c)
        load("amp", amp_hbm, amp, 5)
        load("lad", lad_hbm, lbuf, 6)
        load("itg", itg_hbm, itg, 7)
        load("his", his_hbm, his, 8)
        load("vir", vir_hbm, vir, 9)
        load("of", of_hbm, of_ref, 1)
        load("os", os_hbm, os_ref, 16)

    sends = []
    posted = {}

    def send(key, src, dst, ssem, rsem, device):
        copy = pltpu.make_async_remote_copy(
            src_ref=src, dst_ref=dst, send_sem=ssem, recv_sem=rsem, device_id=device, device_id_type=MESH
        )
        copy.start()
        sends.append(copy)
        posted[key] = copy

    ring_axis = ("z", "y")
    ring_pos = (z, y)
    chunk_pos = (y, z)

    def places(cls, ring_offset, c):
        ring = lax.rem(ring_pos[cls] + ring_offset, 4)
        chunk = lax.rem(chunk_pos[cls] + CHUNKS[c], 4)
        return (ring, chunk) if cls == 0 else (chunk, ring)

    def x_first(cls, c):
        return cls == 1 and c == 3

    def whole(cls, i, ring_offset, c):
        zp, yp = places(cls, ring_offset, c)
        return part.at[pl.ds(2 * cls, 2), i, zp, xh if x_first(cls, c) else slice(None), yp]

    def landing(cls, kind, c):
        return r1.at[cls, kind, c, :, 0] if x_first(cls, c) else r1.at[cls, kind, c]

    def first_pair():
        send("f", part.at[pl.ds(2, 2), :, z, 1 - xh], rf, sx.at[1, 3], qx.at[1, 3], along("x", 2))

    def first_pair_end():
        posted["f"].wait_recv()
        part[pl.ds(2, 2), :, z, xh] += rf[...]

    def own_x(cls, i, c):
        zp, yp = places(cls, 0, c)
        return part.at[pl.ds(2 * cls, 2), i, zp, xh, yp]

    def ring_send(cls, kind, c, i, ring_offset, step):
        send(("r", cls, kind, c), whole(cls, i, ring_offset, c), landing(cls, kind, c),
             s1.at[cls, kind, c], q1.at[cls, kind, c], along(ring_axis[cls], step))

    def m1(cls, c):
        ring_send(cls, 0, c, 0, 2, 1)
        ring_send(cls, 1, c, 1, 2, 3)

    def m1_one(j):
        zp = lax.rem(z + 2, 4)
        for i, step in ((0, 1), (1, 3)):
            send(("h", i, j), part.at[j, i, zp], r0.at[i, j], s0.at[i, j], q0.at[i, j], along("z", step))

    def early(cls, i, c, zp, yp):
        if cls == 1:
            posted["r", cls, i, c].wait_recv()
            ref = whole(cls, i, 1 + 2 * i, c)
            ref[...] += landing(cls, i, c)[...]
            return
        for j in range(2):
            if c == 0:
                posted["h", i, j].wait_recv()
            part[j, i, zp, :, yp] += r0[i, j, :, yp]

    def m2_up(cls, c):
        ring_send(cls, 2, c, 1, 1, 1)

    def m2_down(cls, c):
        ring_send(cls, 3, c, 0, 3, 3)

    def m3_up(cls, c):
        early(cls, 0, c, *places(cls, 1, c))
        ring_send(cls, 4, c, 0, 1, 1)

    def m3_down(cls, c):
        early(cls, 1, c, *places(cls, 3, c))
        ring_send(cls, 5, c, 1, 3, 3)

    def ring_end(cls, c):
        for kind in (2, 3, 4, 5):
            posted["r", cls, kind, c].wait_recv()
        first = whole(cls, 0, 0, c)
        first[...] += landing(cls, 4, c)[...] + landing(cls, 3, c)[...]
        second = whole(cls, 1, 0, c)
        second[...] += landing(cls, 2, c)[...] + landing(cls, 5, c)[...]
        if x_first(cls, c):
            return
        zp, yp = places(cls, 0, c)
        send(("x", cls, c), part.at[pl.ds(2 * cls, 2), :, zp, 1 - xh, yp], rx.at[cls, c],
             sx.at[cls, c], qx.at[cls, c], along("x", 2))

    def pair_end(cls, c):
        if x_first(cls, c):
            return
        posted["x", cls, c].wait_recv()
        zp, yp = places(cls, 0, c)
        ref = part.at[pl.ds(2 * cls, 2), :, zp, xh, yp]
        ref[...] += rx[cls, c]

    def late_send(cls, kind, c, i, step):
        send(("l", cls, kind), own_x(cls, i, c), r3.at[cls, kind], s3.at[cls, kind], q3.at[cls, kind],
             along(ring_axis[1 - cls], step))

    def late0(cls):
        pair_end(cls, 0)
        late_send(cls, 0, 0, 0, 1)
        late_send(cls, 1, 0, 1, 3)

    def late1(cls):
        pair_end(cls, 1)
        late_send(cls, 2, 1, 1, 1)
        posted["l", cls, 0].wait_recv()
        ref = own_x(cls, 0, 1)
        ref[...] += r3[cls, 0]
        late_send(cls, 4, 1, 0, 1)

    def late2(cls):
        pair_end(cls, 2)
        late_send(cls, 3, 2, 0, 3)
        posted["l", cls, 1].wait_recv()
        ref = own_x(cls, 1, 2)
        ref[...] += r3[cls, 1]
        late_send(cls, 5, 2, 1, 3)

    def late3(cls):
        pair_end(cls, 3)
        for kind in (2, 3, 4, 5):
            posted["l", cls, kind].wait_recv()
        first = own_x(cls, 0, 3)
        first[...] += r3[cls, 4] + r3[cls, 3]
        second = own_x(cls, 1, 3)
        second[...] += r3[cls, 2] + r3[cls, 5]

    def relayout(c, b):
        def body(t, carry):
            k0 = pl.multiple_of(t * 64, 64)
            wbuf[b, :, pl.ds(k0, 64), :] = jnp.swapaxes(mbuf[c, pl.ds(k0, 64)], 0, 1)
            return carry

        steps = DEPTH // 64
        if c:
            loads["m", c].wait()
            lax.fori_loop(0, steps, body, 0)
            return
        for q in range(4):
            loads["q", q].wait()
            lax.fori_loop(q * steps // 4, (q + 1) * steps // 4, body, 0)

    def product(c, b, first, count=2):
        zp = lax.rem(z + CHUNKS[c], 4)

        def body(j, carry):
            for i in range(NI):
                got = lax.dot_general(wbuf[b, j], ubuf[i], (((0,), (0,)), ((), ())), preferred_element_type=F32)
                part[j, i, zp] = got.reshape(2, 4, 32, 256)
            return carry

        lax.fori_loop(first, first + count, body, 0)

    def ladder_part(s):
        if s == 0:
            loads["amp"].wait()
            loads["lad"].wait()
        rounded = amp[...].reshape(256, 256).astype(jnp.bfloat16)
        row = lax.broadcasted_iota(jnp.int32, (32, 256), 0)
        lane = lax.broadcasted_iota(jnp.int32, (32, 256), 1)
        same = jnp.where(lax.rem(lane, 32) == row, 1.0, 0.0).astype(F32)

        def body(t, carry):
            r0_ = pl.multiple_of(t * 16, 16)
            ints = lbuf[pl.ds(r0_, 16), s].reshape(512, 256)
            full = lax.dot_general(ints, rounded, (((1,), (1,)), ((), ())), preferred_element_type=F32)
            lgrp[s, pl.ds(r0_, 16), :] = jnp.sum(full.reshape(16, 32, 256) * same[None], axis=1)
            return carry

        lax.fori_loop(0, 4, body, 0)

    def ladder_lanes():
        group = lax.broadcasted_iota(jnp.int32, (256, 128), 0) // 32
        slot = lax.broadcasted_iota(jnp.int32, (256, 128), 1)
        pick = jnp.where(group == slot, 1.0, 0.0).astype(F32)
        lsum[...] = jnp.dot(
            lgrp[...].reshape(256, 256), pick, precision=lax.Precision.HIGHEST, preferred_element_type=F32
        ).reshape(4, 4, 2, 8, 128)
        for d in range(1, 8):
            xd = lax.rem(xpos + d // 2, 4)
            cd = lax.rem(core + d % 2, 2)
            pltpu.make_async_remote_copy(
                src_ref=lsum.at[lax.rem(xd, 2) * 2 + cd, :, xd // 2], dst_ref=lrecv_a.at[d - 1],
                send_sem=sl.at[0], recv_sem=ql.at[0], device_id=at(z, y, xd, cd), device_id_type=MESH,
            ).start()

    def arrivals(ref, n):
        return pltpu.make_async_remote_copy(
            src_ref=ref, dst_ref=ref, send_sem=sl.at[n], recv_sem=ql.at[n], device_id=plane[0], device_id_type=MESH
        )

    def ladder_plane():
        arrivals(lrecv_a, 0).wait_recv()
        lplane[...] = lsum[narrow, :, xh] + jnp.sum(lrecv_a[...], axis=0)
        for d in range(1, 16):
            pltpu.make_async_remote_copy(
                src_ref=lplane.at[lax.rem(z + d // 4, 4)], dst_ref=lrecv_b.at[d - 1],
                send_sem=sl.at[1], recv_sem=ql.at[1], device_id=plane[d - 1], device_id_type=MESH,
            ).start()

    def ladder_end():
        arrivals(lrecv_b, 1).wait_recv()
        total = lplane[z] + jnp.sum(lrecv_b[...], axis=0)
        row = lax.broadcasted_iota(jnp.int32, (8, 128), 0)
        return [jnp.sum(jnp.where(row == 2 * y + e, total, 0.0), axis=0, keepdims=True) for e in range(2)]

    def fold(x):
        eight = jnp.sum(x.reshape(4, 8, 256), axis=0)
        return eight[:, :128] + eight[:, 128:]

    def tail(cls, ladder_rows, sums):
        row = lax.broadcasted_iota(jnp.int32, (32, 256), 0)
        lane = lax.broadcasted_iota(jnp.int32, (32, 256), 1)
        lane1 = lax.broadcasted_iota(jnp.int32, (1, 128), 1)
        lanes = lax.broadcasted_iota(jnp.int32, (32, 128), 1)
        rows = lax.broadcasted_iota(jnp.int32, (32, 128), 0)
        block = vir[:, pl.ds(pl.multiple_of(wide // 4 * 128, 128), 128)]
        down = jnp.sum(jnp.where(lanes == lax.rem(wide, 4) * 32 + rows, block, 0.0), axis=1, keepdims=True)
        across = vir[:, pl.ds(pl.multiple_of(narrow * 256, 256), 256)]
        for j in (2 * cls, 2 * cls + 1):
            for i in range(NI):
                ij = i * NJ + j
                placed = jnp.zeros((32, 256), F32)
                for e in range(2):
                    one = jnp.sum(jnp.where(lane1 == ij, ladder_rows[e], 0.0), axis=1, keepdims=True)
                    placed = jnp.where((row == e) & (lane == 0), one, placed)
                denominator = down + across - of_ref[:, i : i + 1] - os_ref[:, j : j + 1]
                a = amp[i, j]
                v = itg[i, j]
                r = v + part[j, i, z, xh, y] + placed - denominator * a
                new = a + r / denominator
                res[i, j] = r
                upd[i, j] = new
                terms = [new * v] + [his[h, i, j] * r for h in range(4)] + [r * r]
                sums = [s + fold(t) for s, t in zip(sums, terms)]
        return sums

    def paced(*keys):
        for key in keys:
            sends.remove(posted[key])
            posted[key].wait_send()

    def paced_ring(cls, c, *kinds):
        paced(*[("r", cls, kind, c) for kind in kinds])

    relayout(0, 0)
    loads["u"].wait()
    load_rest()
    product(0, 0, 0, 1)
    pl.semaphore_wait(barrier, len(plane + row_of_chips))
    m1_one(0)
    product(0, 0, 1, 1)
    m1_one(1)
    product(0, 0, 2)
    m1(1, 0)
    relayout(3, 0)
    product(3, 0, 2)
    first_pair()
    m2_up(1, 0)
    m2_down(1, 0)
    relayout(1, 1)
    product(1, 1, 0)
    m3_up(1, 0)
    m3_down(1, 0)
    product(1, 1, 2)
    m1(1, 1)
    m2_up(0, 0)
    relayout(2, 1)
    product(2, 1, 0)
    m2_down(0, 0)
    m2_up(1, 1)
    m2_down(1, 1)
    product(2, 1, 2)
    ring_end(1, 0)
    m3_up(0, 0)
    m3_down(0, 0)
    product(3, 0, 0)
    m3_up(1, 1)
    m3_down(1, 1)
    m2_up(0, 1)
    m2_down(0, 1)
    ladder_part(0)
    m3_up(0, 1)
    m3_down(0, 1)
    m1(1, 2)
    ladder_part(1)
    ladder_part(2)
    m2_up(1, 2)
    m2_down(1, 2)
    ladder_part(3)
    ladder_lanes()
    ring_end(0, 0)
    m2_up(0, 2)
    m2_down(0, 2)
    ring_end(1, 1)
    first_pair_end()
    m1(1, 3)
    late0(1)
    m3_up(1, 2)
    m3_down(1, 2)
    m3_up(0, 2)
    m3_down(0, 2)
    ring_end(0, 1)
    m2_up(0, 3)
    m2_down(0, 3)
    late0(0)
    m2_up(1, 3)
    m2_down(1, 3)
    late1(1)
    ring_end(1, 2)
    m3_up(1, 3)
    m3_down(1, 3)
    m3_up(0, 3)
    m3_down(0, 3)
    late1(0)
    ladder_plane()
    ring_end(0, 2)
    late2(1)
    late2(0)
    for name in ("itg", "his", "vir", "of", "os"):
        loads[name].wait()
    ring_end(0, 3)
    ring_end(1, 3)
    rows = ladder_end()
    late3(1)
    sums = tail(1, rows, [jnp.zeros((8, 128), F32)] * 6)
    late3(0)
    sums = tail(0, rows, sums)

    lane = lax.broadcasted_iota(jnp.int32, (1, 128), 1)
    mine = jnp.zeros((1, 128), F32)
    for n, s in enumerate(sums):
        one = jnp.sum(jnp.sum(s, axis=0, keepdims=True), axis=1, keepdims=True)
        mine = jnp.where(lane == n, one, mine)

    def everyone(buf, own, row, devices, n):
        count = len(devices)
        buf[own] = row
        for device in devices:
            pltpu.make_async_remote_copy(
                src_ref=buf.at[own], dst_ref=buf.at[own], send_sem=ss.at[n], recv_sem=qs.at[n],
                device_id=device, device_id_type=MESH,
            ).start()
        arrived = pltpu.make_async_remote_copy(
            src_ref=buf.at[pl.ds(0, count)], dst_ref=buf.at[pl.ds(0, count)], send_sem=ss.at[n], recv_sem=qs.at[n],
            device_id=devices[0], device_id_type=MESH,
        )
        arrived.wait_recv()
        return jnp.sum(buf[...], axis=0), arrived

    def totals():
        row, first = everyone(sums_a, z * 4 + y, mine, plane, 0)
        row, second = everyone(sums_b, xpos * 2 + core, row, row_of_chips, 1)
        row = row * (1.0 / 8388608.0)
        ene_ref[0] = row[0, 0]
        for n in range(5):
            int_ref[n] = row[0, n + 1]
        first.wait_send()
        second.wait_send()

    totals()
    arrivals(lrecv_a, 0).wait_send()
    arrivals(lrecv_b, 1).wait_send()
    for copy in sends:
        copy.wait_send()


def shards(amplitudes, cycle_amps, cycle_ints, ladder_ints, integrals, history, vir_energy, occ_first, occ_second):
    smem = pl.BlockSpec(memory_space=pltpu.SMEM)
    bf16 = jnp.bfloat16
    dma = pltpu.SemaphoreType.DMA
    block = pltpu.VMEM((NI, NJ, 32, 256), F32)
    vmem = pl.BlockSpec(memory_space=pltpu.VMEM)
    return pl.pallas_call(
        kernel,
        out_shape=(block, block, jax.ShapeDtypeStruct((1,), F32), jax.ShapeDtypeStruct((5,), F32)),
        in_specs=[pl.BlockSpec(memory_space=pltpu.HBM)] * 9,
        out_specs=(vmem, vmem, smem, smem),
        scratch_shapes=[
            pltpu.VMEM((4, DEPTH, 4, 256), bf16),
            pltpu.VMEM((NI, DEPTH, 256), bf16),
            pltpu.VMEM((2, 4, DEPTH, 256), bf16),
            pltpu.VMEM((NJ, NI, 4, 2, 4, 32, 256), F32),
            pltpu.VMEM((2, 2, 2, 4, 32, 256), F32),
            pltpu.VMEM((2, 6, 4, 2, 2, 32, 256), F32),
            pltpu.VMEM((2, 4, 2, 2, 32, 256), F32),
            pltpu.VMEM((2, 2, 4, 32, 256), F32),
            pltpu.VMEM((2, 6, 2, 32, 256), F32),
            pltpu.VMEM((64, 4, 32, 256), bf16),
            pltpu.VMEM((4, 64, 256), F32),
            pltpu.VMEM((4, 4, 2, 8, 128), F32),
            pltpu.VMEM((7, 4, 8, 128), F32),
            pltpu.VMEM((4, 8, 128), F32),
            pltpu.VMEM((15, 8, 128), F32),
            pltpu.VMEM((NI, NJ, 32, 256), F32),
            pltpu.VMEM((NI, NJ, 32, 256), F32),
            pltpu.VMEM((4, NI, NJ, 32, 256), F32),
            pltpu.VMEM((1, 1024), F32),
            pltpu.VMEM((1, NI), F32),
            pltpu.VMEM((1, NJ), F32),
            pltpu.VMEM((16, 1, 128), F32),
            pltpu.VMEM((8, 1, 128), F32),
            dma((17,)),
            dma((2, 2)), dma((2, 2)),
            dma((2, 6, 4)), dma((2, 6, 4)),
            dma((2, 4)), dma((2, 4)),
            dma((2, 6)), dma((2, 6)),
            dma((2,)), dma((2,)),
            dma((2,)), dma((2,)),
        ],
        compiler_params=pltpu.CompilerParams(
            collective_id=0, has_side_effects=True, vmem_limit_bytes=52 * 2**20
        ),
        cost_estimate=pl.CostEstimate(flops=9 * 10**9, bytes_accessed=27 * 10**6, transcendentals=0),
        name="window",
    )(*(pltpu.with_memory_space_constraint(x, pltpu.HBM) for x in (
        amplitudes,
        cycle_amps.reshape(NI, DEPTH, 256),
        cycle_ints.reshape(DEPTH, 4, 1024),
        ladder_ints,
        integrals,
        history,
        vir_energy.reshape(1, 1024),
        occ_first.reshape(1, NI),
        occ_second.reshape(1, NJ),
    )))


def solution(mesh):
    spread = P(None, None, "wide", "narrow")
    return jax.shard_map(
        shards,
        mesh=mesh,
        in_specs=(
            spread,
            spread,
            P(None, "wide", None, None),
            spread,
            spread,
            P(None, None, None, "wide", "narrow"),
            P(),
            P(),
            P(),
        ),
        out_specs=(spread, spread, P(), P()),
        check_vma=False,
    )
```

time: 88.1 us -> 68.7 us (0.78)
  Pallas kernels: 80.3 us -> 64.4 us
  local copies, waits for them, and re-layouts: 4.52 us -> 1.92 us
    pallas_call x1, Pallas kernels: 80.3 us -> 64.4 us  [shards(): pl.pallas_call(kernel, out_shape=(block, block, jax.ShapeDtypeStruct((1,)...]
    unnamed x3, local copies, waits for them, and re-layouts: 4.52 us -> 1.92 us
where the time goes in v2:
time: 68.7 us; the launch traced here: 68.6 us
  Pallas kernels  64.4 us (94%)
  between operations  2.34 us (3%)
  local copies, waits for them, and re-layouts  1.92 us (3%)
    pallas_call x1, Pallas kernels, shards(): pl.pallas_call(kernel, out_shape=(block, block, jax.ShapeDtypeStruct((1,)...  64.4 us
    unnamed x3, local copies, waits for them, and re-layouts  1.92 us

profile of v2, /device:TPU:1, one launch (start us, length us, event | category | flops | bytes accessed | tf_op | source)
XLA Modules:
  0.0 68.6 jit_solution(9181316068348648008)
XLA Ops:
  0.6 64.4 %window.1 = (f32[2,4,32,256]{3,2,1,0:T(8,128)S(1)}, f32[2,4,32,256]{3,2,1,0:T(8,128)S(1)}, f32[1]{0:T(128)}, f32[5]{0:T(128)S(1)}) custom-call(f32[2,4,32,256]{3,2,1,0:T(8,128)} %amp_hbm.1, bf16[2,2048,256]{2,1,0:T(8,128)(2,1)} %bitcast.6, bf16[2048,4,1024]{2,1,0:T(4,128)(2,1)} %bitcast.5, bf16[64,4,32,256]{3,2,1,0:T(8,128)(2,1)} %lad_hbm.1, ...), custom_call_target="tpu_custom_call" | custom-call | flops 8999999488 | bytes 27000000 | tf_op jit(solution)/shard_map/window/pallas_call | solution.py:458
  65.0 0.7 %copy.17 = f32[2,4,32,256]{3,2,1,0:T(8,128)} copy(f32[2,4,32,256]{3,2,1,0:T(8,128)S(1)} %get-tuple-element.4) | data formatting | bytes 524288
  65.7 0.7 %copy.18 = f32[2,4,32,256]{3,2,1,0:T(8,128)} copy(f32[2,4,32,256]{3,2,1,0:T(8,128)S(1)} %get-tuple-element.5) | data formatting | bytes 524288
  67.0 0.5 copy.20

commit v3 on v2

--- a/solution.py
+++ b/solution.py
@@ -15,11 +15,11 @@
 
 def kernel(
     amp_hbm, u_hbm, m_hbm, lad_hbm, itg_hbm, his_hbm, vir_hbm, of_hbm, os_hbm,
-    upd, res, ene_ref, int_ref,
+    both_ref, tot_ref,
     mbuf, ubuf, wbuf, part, r0, r1, rx, rf, r3,
     lbuf, lgrp, lsum, lrecv_a, lplane, lrecv_b,
     amp, itg, his, vir, of_ref, os_ref, sums_a, sums_b,
-    lsem, s0, q0, s1, q1, sx, qx, s3, q3, sl, ql, ss, qs,
+    lsem, sent, q0, q1, qe, qx, q3, qf, sl, ql, ss, qs,
 ):
     wide = lax.axis_index("wide")
     narrow = lax.axis_index("narrow")
@@ -75,16 +75,19 @@
         load("of", of_hbm, of_ref, 1)
         load("os", os_hbm, os_ref, 16)
 
-    sends = []
-    posted = {}
-
-    def send(key, src, dst, ssem, rsem, device):
-        copy = pltpu.make_async_remote_copy(
-            src_ref=src, dst_ref=dst, send_sem=ssem, recv_sem=rsem, device_id=device, device_id_type=MESH
-        )
-        copy.start()
-        sends.append(copy)
-        posted[key] = copy
+    def send(src, dst, group, rsem, device):
+        pltpu.make_async_remote_copy(
+            src_ref=src, dst_ref=dst, send_sem=sent.at[group], recv_sem=rsem, device_id=device, device_id_type=MESH
+        ).start()
+
+    def all_sent():
+        groups = (r0, r1.at[0, pl.ds(2, 4)], r1.at[1, :, pl.ds(0, 3)], r1.at[1, :, 3, :, 0],
+                  rx.at[0], rx.at[1, pl.ds(0, 3)], rf, r3.at[0], r3.at[1])
+        for group, ref in enumerate(groups):
+            pltpu.make_async_remote_copy(
+                src_ref=ref, dst_ref=ref, send_sem=sent.at[group], recv_sem=q0.at[0], device_id=plane[0],
+                device_id_type=MESH,
+            ).wait_send()
 
     ring_axis = ("z", "y")
     ring_pos = (z, y)
@@ -92,33 +95,41 @@
 
     def places(cls, ring_offset, c):
         ring = lax.rem(ring_pos[cls] + ring_offset, 4)
-        chunk = lax.rem(chunk_pos[cls] + CHUNKS[c], 4)
+        chunk = lax.rem(chunk_pos[cls] + CHUNKS[min(c, 3)], 4)
         return (ring, chunk) if cls == 0 else (chunk, ring)
+
+    def js(cls, c):
+        return pl.ds(c - 3, 1) if cls == 0 and c >= 3 else pl.ds(2 * cls, 2)
 
     def x_first(cls, c):
         return cls == 1 and c == 3
 
     def whole(cls, i, ring_offset, c):
         zp, yp = places(cls, ring_offset, c)
-        return part.at[pl.ds(2 * cls, 2), i, zp, xh if x_first(cls, c) else slice(None), yp]
+        return part.at[js(cls, c), i, zp, xh if x_first(cls, c) else slice(None), yp]
 
     def landing(cls, kind, c):
-        return r1.at[cls, kind, c, :, 0] if x_first(cls, c) else r1.at[cls, kind, c]
+        if x_first(cls, c):
+            return r1.at[cls, kind, c, :, 0]
+        if cls == 0 and c >= 3:
+            return r1.at[cls, kind, 3, js(cls, c)]
+        return r1.at[cls, kind, c]
+
+    def wait_bytes(ref, sem):
+        pltpu.make_async_remote_copy(
+            src_ref=ref, dst_ref=ref, send_sem=sent.at[0], recv_sem=sem, device_id=plane[0], device_id_type=MESH
+        ).wait_recv()
 
     def first_pair():
-        send("f", part.at[pl.ds(2, 2), :, z, 1 - xh], rf, sx.at[1, 3], qx.at[1, 3], along("x", 2))
+        send(part.at[pl.ds(2, 2), :, z, 1 - xh], rf, 6, qf.at[0], along("x", 2))
 
     def first_pair_end():
-        posted["f"].wait_recv()
+        wait_bytes(rf, qf.at[0])
         part[pl.ds(2, 2), :, z, xh] += rf[...]
 
-    def own_x(cls, i, c):
-        zp, yp = places(cls, 0, c)
-        return part.at[pl.ds(2 * cls, 2), i, zp, xh, yp]
-
     def ring_send(cls, kind, c, i, ring_offset, step):
-        send(("r", cls, kind, c), whole(cls, i, ring_offset, c), landing(cls, kind, c),
-             s1.at[cls, kind, c], q1.at[cls, kind, c], along(ring_axis[cls], step))
+        send(whole(cls, i, ring_offset, c), landing(cls, kind, c), 2 + x_first(cls, c) if cls else 1,
+             q1.at[kind, c] if kind < 2 else qe.at[cls, c], along(ring_axis[cls], step))
 
     def m1(cls, c):
         ring_send(cls, 0, c, 0, 2, 1)
@@ -127,18 +138,17 @@
     def m1_one(j):
         zp = lax.rem(z + 2, 4)
         for i, step in ((0, 1), (1, 3)):
-            send(("h", i, j), part.at[j, i, zp], r0.at[i, j], s0.at[i, j], q0.at[i, j], along("z", step))
-
-    def early(cls, i, c, zp, yp):
+            send(part.at[j, i, zp], r0.at[i, j], 0, q0.at[i], along("z", step))
+
+    def early(cls, i, c):
+        ref = whole(cls, i, 1 + 2 * i, c)
         if cls == 1:
-            posted["r", cls, i, c].wait_recv()
-            ref = whole(cls, i, 1 + 2 * i, c)
+            wait_bytes(landing(cls, i, c), q1.at[i, c])
             ref[...] += landing(cls, i, c)[...]
             return
-        for j in range(2):
-            if c == 0:
-                posted["h", i, j].wait_recv()
-            part[j, i, zp, :, yp] += r0[i, j, :, yp]
+        if c == 0:
+            wait_bytes(r0.at[i], q0.at[i])
+        ref[...] += r0[i, js(cls, c), :, places(cls, 0, c)[1]]
 
     def m2_up(cls, c):
         ring_send(cls, 2, c, 1, 1, 1)
@@ -147,16 +157,20 @@
         ring_send(cls, 3, c, 0, 3, 3)
 
     def m3_up(cls, c):
-        early(cls, 0, c, *places(cls, 1, c))
+        early(cls, 0, c)
         ring_send(cls, 4, c, 0, 1, 1)
 
     def m3_down(cls, c):
-        early(cls, 1, c, *places(cls, 3, c))
+        early(cls, 1, c)
         ring_send(cls, 5, c, 1, 3, 3)
 
     def ring_end(cls, c):
-        for kind in (2, 3, 4, 5):
-            posted["r", cls, kind, c].wait_recv()
+        if x_first(cls, c):
+            wait_bytes(r1.at[cls, pl.ds(2, 4), c, :, 0], qe.at[cls, c])
+        elif cls == 0 and c >= 3:
+            wait_bytes(r1.at[cls, pl.ds(2, 4), 3, js(cls, c)], qe.at[cls, c])
+        else:
+            wait_bytes(r1.at[cls, pl.ds(2, 4), c], qe.at[cls, c])
         first = whole(cls, 0, 0, c)
         first[...] += landing(cls, 4, c)[...] + landing(cls, 3, c)[...]
         second = whole(cls, 1, 0, c)
@@ -164,20 +178,25 @@
         if x_first(cls, c):
             return
         zp, yp = places(cls, 0, c)
-        send(("x", cls, c), part.at[pl.ds(2 * cls, 2), :, zp, 1 - xh, yp], rx.at[cls, c],
-             sx.at[cls, c], qx.at[cls, c], along("x", 2))
+        send(part.at[js(cls, c), :, zp, 1 - xh, yp], paired(cls, c), 4 + cls, qx.at[cls, c], along("x", 2))
+
+    def paired(cls, c):
+        return rx.at[cls, 3, js(cls, c)] if cls == 0 and c >= 3 else rx.at[cls, c]
 
     def pair_end(cls, c):
         if x_first(cls, c):
             return
-        posted["x", cls, c].wait_recv()
+        wait_bytes(paired(cls, c), qx.at[cls, c])
         zp, yp = places(cls, 0, c)
-        ref = part.at[pl.ds(2 * cls, 2), :, zp, xh, yp]
-        ref[...] += rx[cls, c]
+        ref = part.at[js(cls, c), :, zp, xh, yp]
+        ref[...] += paired(cls, c)[...]
+
+    def own_x(cls, i, c):
+        zp, yp = places(cls, 0, c)
+        return part.at[pl.ds(2 * cls, 2), i, zp, xh, yp]
 
     def late_send(cls, kind, c, i, step):
-        send(("l", cls, kind), own_x(cls, i, c), r3.at[cls, kind], s3.at[cls, kind], q3.at[cls, kind],
-             along(ring_axis[1 - cls], step))
+        send(own_x(cls, i, c), r3.at[cls, kind], 7 + cls, q3.at[cls, min(kind, 2)], along(ring_axis[1 - cls], step))
 
     def late0(cls):
         pair_end(cls, 0)
@@ -187,7 +206,7 @@
     def late1(cls):
         pair_end(cls, 1)
         late_send(cls, 2, 1, 1, 1)
-        posted["l", cls, 0].wait_recv()
+        wait_bytes(r3.at[cls, 0], q3.at[cls, 0])
         ref = own_x(cls, 0, 1)
         ref[...] += r3[cls, 0]
         late_send(cls, 4, 1, 0, 1)
@@ -195,15 +214,16 @@
     def late2(cls):
         pair_end(cls, 2)
         late_send(cls, 3, 2, 0, 3)
-        posted["l", cls, 1].wait_recv()
+        wait_bytes(r3.at[cls, 1], q3.at[cls, 1])
         ref = own_x(cls, 1, 2)
         ref[...] += r3[cls, 1]
         late_send(cls, 5, 2, 1, 3)
 
     def late3(cls):
+        wait_bytes(r3.at[cls, pl.ds(2, 4)], q3.at[cls, 2])
         pair_end(cls, 3)
-        for kind in (2, 3, 4, 5):
-            posted["l", cls, kind].wait_recv()
+        if cls == 0:
+            pair_end(cls, 4)
         first = own_x(cls, 0, 3)
         first[...] += r3[cls, 4] + r3[cls, 3]
         second = own_x(cls, 1, 3)
@@ -313,19 +333,11 @@
                 v = itg[i, j]
                 r = v + part[j, i, z, xh, y] + placed - denominator * a
                 new = a + r / denominator
-                res[i, j] = r
-                upd[i, j] = new
+                both_ref[1, i, j] = r
+                both_ref[0, i, j] = new
                 terms = [new * v] + [his[h, i, j] * r for h in range(4)] + [r * r]
                 sums = [s + fold(t) for s, t in zip(sums, terms)]
         return sums
-
-    def paced(*keys):
-        for key in keys:
-            sends.remove(posted[key])
-            posted[key].wait_send()
-
-    def paced_ring(cls, c, *kinds):
-        paced(*[("r", cls, kind, c) for kind in kinds])
 
     relayout(0, 0)
     loads["u"].wait()
@@ -364,16 +376,16 @@
     m2_up(0, 1)
     m2_down(0, 1)
     ladder_part(0)
+    m1(1, 2)
+    ladder_part(1)
     m3_up(0, 1)
     m3_down(0, 1)
-    m1(1, 2)
-    ladder_part(1)
     ladder_part(2)
+    ring_end(0, 0)
     m2_up(1, 2)
     m2_down(1, 2)
     ladder_part(3)
     ladder_lanes()
-    ring_end(0, 0)
     m2_up(0, 2)
     m2_down(0, 2)
     ring_end(1, 1)
@@ -382,28 +394,33 @@
     late0(1)
     m3_up(1, 2)
     m3_down(1, 2)
+    ring_end(0, 1)
     m3_up(0, 2)
     m3_down(0, 2)
-    ring_end(0, 1)
+    late0(0)
     m2_up(0, 3)
     m2_down(0, 3)
-    late0(0)
+    m2_up(0, 4)
+    m2_down(0, 4)
+    late1(1)
+    m3_up(0, 3)
+    m3_down(0, 3)
+    ring_end(1, 2)
     m2_up(1, 3)
     m2_down(1, 3)
-    late1(1)
-    ring_end(1, 2)
     m3_up(1, 3)
     m3_down(1, 3)
-    m3_up(0, 3)
-    m3_down(0, 3)
+    m3_up(0, 4)
+    m3_down(0, 4)
     late1(0)
+    ring_end(0, 2)
     ladder_plane()
-    ring_end(0, 2)
     late2(1)
     late2(0)
     for name in ("itg", "his", "vir", "of", "os"):
         loads[name].wait()
     ring_end(0, 3)
+    ring_end(0, 4)
     ring_end(1, 3)
     rows = ladder_end()
     late3(1)
@@ -435,31 +452,26 @@
     def totals():
         row, first = everyone(sums_a, z * 4 + y, mine, plane, 0)
         row, second = everyone(sums_b, xpos * 2 + core, row, row_of_chips, 1)
-        row = row * (1.0 / 8388608.0)
-        ene_ref[0] = row[0, 0]
-        for n in range(5):
-            int_ref[n] = row[0, n + 1]
+        tot_ref[...] = row * (1.0 / 8388608.0)
         first.wait_send()
         second.wait_send()
 
     totals()
     arrivals(lrecv_a, 0).wait_send()
     arrivals(lrecv_b, 1).wait_send()
-    for copy in sends:
-        copy.wait_send()
+    all_sent()
 
 
 def shards(amplitudes, cycle_amps, cycle_ints, ladder_ints, integrals, history, vir_energy, occ_first, occ_second):
-    smem = pl.BlockSpec(memory_space=pltpu.SMEM)
     bf16 = jnp.bfloat16
     dma = pltpu.SemaphoreType.DMA
-    block = pltpu.VMEM((NI, NJ, 32, 256), F32)
+    block = pltpu.VMEM((2, NI, NJ, 32, 256), F32)
     vmem = pl.BlockSpec(memory_space=pltpu.VMEM)
-    return pl.pallas_call(
+    stacked, totals = pl.pallas_call(
         kernel,
-        out_shape=(block, block, jax.ShapeDtypeStruct((1,), F32), jax.ShapeDtypeStruct((5,), F32)),
+        out_shape=(block, pltpu.VMEM((1, 128), F32)),
         in_specs=[pl.BlockSpec(memory_space=pltpu.HBM)] * 9,
-        out_specs=(vmem, vmem, smem, smem),
+        out_specs=(vmem, vmem),
         scratch_shapes=[
             pltpu.VMEM((4, DEPTH, 4, 256), bf16),
             pltpu.VMEM((NI, DEPTH, 256), bf16),
@@ -485,10 +497,13 @@
             pltpu.VMEM((16, 1, 128), F32),
             pltpu.VMEM((8, 1, 128), F32),
             dma((17,)),
-            dma((2, 2)), dma((2, 2)),
-            dma((2, 6, 4)), dma((2, 6, 4)),
-            dma((2, 4)), dma((2, 4)),
-            dma((2, 6)), dma((2, 6)),
+            dma((9,)),
+            dma((2,)),
+            dma((2, 4)),
+            dma((2, 5)),
+            dma((2, 5)),
+            dma((2, 3)),
+            dma((1,)),
             dma((2,)), dma((2,)),
             dma((2,)), dma((2,)),
         ],
@@ -508,6 +523,7 @@
         occ_first.reshape(1, NI),
         occ_second.reshape(1, NJ),
     )))
+    return stacked[0], stacked[1], totals[0, :1], totals[0, 1:6]
 
 
 def solution(mesh):

time: 68.7 us -> 65.2 us (0.949)
  Pallas kernels: 64.4 us -> 61.8 us
    pallas_call x1, Pallas kernels: 64.4 us -> 61.8 us  [shards(): pl.pallas_call(kernel, out_shape=(block, pltpu.VMEM((1, 128), F32)), in_s...]
    unnamed x3 -> x0, local copies, waits for them, and re-layouts: 1.92 us -> none
    squeeze x0 -> x2, local copies, waits for them, and re-layouts: none -> 1.42 us  [shards(): return (stacked[0], stacked[1], totals[0, :1], totals[0, 1:6])]
where the time goes in v3:
time: 65.2 us; the launch traced here: 65.1 us
  Pallas kernels  61.8 us (95%)
  between operations  1.81 us (3%)
  local copies, waits for them, and re-layouts  1.42 us (2%)
    pallas_call x1, Pallas kernels, shards(): pl.pallas_call(kernel, out_shape=(block, pltpu.VMEM((1, 128), F32)), in_s...  61.8 us
    squeeze x2, local copies, waits for them, and re-layouts, shards(): return (stacked[0], stacked[1], totals[0, :1], totals[0, 1:6])  1.42 us

profile of v3, /device:TPU:1, one launch (start us, length us, event | category | flops | bytes accessed | tf_op | source)
XLA Modules:
  0.0 65.1 jit_solution(15348997486976552399)
XLA Ops:
  0.6 61.8 %window.1 = (f32[2,2,4,32,256]{4,3,2,1,0:T(8,128)S(1)}, f32[1,128]{1,0:T(1,128)S(1)}) custom-call(f32[2,4,32,256]{3,2,1,0:T(8,128)} %amp_hbm.1, bf16[2,2048,256]{2,1,0:T(8,128)(2,1)} %bitcast.15, bf16[2048,4,1024]{2,1,0:T(4,128)(2,1)} %bitcast.14, bf16[64,4,32,256]{3,2,1,0:T(8,128)(2,1)} %lad_hbm.1, f32[2,4,32,256]{3,2,1,0:T(8,128)} %itg_hbm.1, ...), custom_call_target="tpu_custom_call" | custom-call | flops 8999999488 | bytes 27000000 | tf_op jit(solution)/shard_map/window/pallas_call | solution.py:470
  62.5 0.8 %slice_bitcast_fusion = (f32[2,4,32,256]{3,2,1,0:T(8,128)}, f32[2,4,32,256]{3,2,1,0:T(8,128)}) fusion(f32[2,2,4,32,256]{4,3,2,1,0:T(8,128)S(1)} %get-tuple-element.6), kind=kLoop, calls=%fused_computation | loop fusion | bytes 1048576 | tf_op jit(solution)/shard_map/squeeze | solution.py:526
  63.3 0.6 slice_bitcast_fusion.2

commit v4 on v3

--- a/solution.py
+++ b/solution.py
@@ -16,7 +16,7 @@
 def kernel(
     amp_hbm, u_hbm, m_hbm, lad_hbm, itg_hbm, his_hbm, vir_hbm, of_hbm, os_hbm,
     both_ref, tot_ref,
-    mbuf, ubuf, wbuf, part, r0, r1, rx, rf, r3,
+    mbuf, ubuf, wbuf, part, r0, r1, rx, rf, rg, r3,
     lbuf, lgrp, lsum, lrecv_a, lplane, lrecv_b,
     amp, itg, his, vir, of_ref, os_ref, sums_a, sums_b,
     lsem, sent, q0, q1, qe, qx, q3, qf, sl, ql, ss, qs,
@@ -81,8 +81,13 @@
         ).start()
 
     def all_sent():
-        groups = (r0, r1.at[0, pl.ds(2, 4)], r1.at[1, :, pl.ds(0, 3)], r1.at[1, :, 3, :, 0],
-                  rx.at[0], rx.at[1, pl.ds(0, 3)], rf, r3.at[0], r3.at[1])
+        rings = [
+            ref
+            for cls, kinds in ((0, pl.ds(2, 4)), (1, pl.ds(0, 6)))
+            for ref in (r1.at[cls, kinds, pl.ds(0, 3)], r1.at[cls, kinds, 3, pl.ds(0, 1)], r1.at[cls, kinds, 3, pl.ds(1, 1), 0])
+        ]
+        pairs = [ref for cls in range(2) for ref in (rx.at[cls, pl.ds(0, 3)], rx.at[cls, 3, pl.ds(0, 1)])]
+        groups = [r0, *rings, *pairs, rf, rg, r3.at[0], r3.at[1]]
         for group, ref in enumerate(groups):
             pltpu.make_async_remote_copy(
                 src_ref=ref, dst_ref=ref, send_sem=sent.at[group], recv_sem=q0.at[0], device_id=plane[0],
@@ -99,21 +104,20 @@
         return (ring, chunk) if cls == 0 else (chunk, ring)
 
     def js(cls, c):
-        return pl.ds(c - 3, 1) if cls == 0 and c >= 3 else pl.ds(2 * cls, 2)
+        return pl.ds(2 * cls + c - 3, 1) if c >= 3 else pl.ds(2 * cls, 2)
 
     def x_first(cls, c):
-        return cls == 1 and c == 3
+        return c == 4
 
     def whole(cls, i, ring_offset, c):
         zp, yp = places(cls, ring_offset, c)
         return part.at[js(cls, c), i, zp, xh if x_first(cls, c) else slice(None), yp]
 
     def landing(cls, kind, c):
-        if x_first(cls, c):
-            return r1.at[cls, kind, c, :, 0]
-        if cls == 0 and c >= 3:
-            return r1.at[cls, kind, 3, js(cls, c)]
-        return r1.at[cls, kind, c]
+        if c < 3:
+            return r1.at[cls, kind, c]
+        place = r1.at[cls, kind, 3, pl.ds(c - 3, 1)]
+        return place.at[:, 0] if x_first(cls, c) else place
 
     def wait_bytes(ref, sem):
         pltpu.make_async_remote_copy(
@@ -121,14 +125,26 @@
         ).wait_recv()
 
     def first_pair():
-        send(part.at[pl.ds(2, 2), :, z, 1 - xh], rf, 6, qf.at[0], along("x", 2))
+        send(part.at[3, :, z, 1 - xh], rf, 11, qf.at[0], along("x", 2))
 
     def first_pair_end():
         wait_bytes(rf, qf.at[0])
-        part[pl.ds(2, 2), :, z, xh] += rf[...]
+        part[3, :, z, xh] += rf[...]
+
+    def second_pair():
+        early(0, 0, 4, True)
+        early(0, 1, 4, True)
+        for n, offset in enumerate((1, 3, 0)):
+            send(part.at[1, :, lax.rem(z + offset, 4), 1 - xh, y], rg.at[n], 12, qf.at[1], along("x", 2))
+
+    def second_pair_end():
+        wait_bytes(rg, qf.at[1])
+        for n, offset in enumerate((1, 3, 0)):
+            part[1, :, lax.rem(z + offset, 4), xh, y] += rg[n]
 
     def ring_send(cls, kind, c, i, ring_offset, step):
-        send(whole(cls, i, ring_offset, c), landing(cls, kind, c), 2 + x_first(cls, c) if cls else 1,
+        group = 1 + 3 * cls + max(c - 2, 0)
+        send(whole(cls, i, ring_offset, c), landing(cls, kind, c), group,
              q1.at[kind, c] if kind < 2 else qe.at[cls, c], along(ring_axis[cls], step))
 
     def m1(cls, c):
@@ -140,7 +156,11 @@
         for i, step in ((0, 1), (1, 3)):
             send(part.at[j, i, zp], r0.at[i, j], 0, q0.at[i], along("z", step))
 
-    def early(cls, i, c):
+    def early(cls, i, c, now=False):
+        if cls == 0 and x_first(cls, c):
+            if now:
+                part[1, i, lax.rem(z + 1 + 2 * i, 4), :, y] += r0[i, 1, :, y]
+            return
         ref = whole(cls, i, 1 + 2 * i, c)
         if cls == 1:
             wait_bytes(landing(cls, i, c), q1.at[i, c])
@@ -165,12 +185,12 @@
         ring_send(cls, 5, c, 1, 3, 3)
 
     def ring_end(cls, c):
-        if x_first(cls, c):
-            wait_bytes(r1.at[cls, pl.ds(2, 4), c, :, 0], qe.at[cls, c])
-        elif cls == 0 and c >= 3:
-            wait_bytes(r1.at[cls, pl.ds(2, 4), 3, js(cls, c)], qe.at[cls, c])
+        if c < 3:
+            wait_bytes(r1.at[cls, pl.ds(2, 4), c], qe.at[cls, c])
+        elif c == 3:
+            wait_bytes(r1.at[cls, pl.ds(2, 4), 3, pl.ds(0, 1)], qe.at[cls, c])
         else:
-            wait_bytes(r1.at[cls, pl.ds(2, 4), c], qe.at[cls, c])
+            wait_bytes(r1.at[cls, pl.ds(2, 4), 3, pl.ds(1, 1), 0], qe.at[cls, c])
         first = whole(cls, 0, 0, c)
         first[...] += landing(cls, 4, c)[...] + landing(cls, 3, c)[...]
         second = whole(cls, 1, 0, c)
@@ -178,10 +198,10 @@
         if x_first(cls, c):
             return
         zp, yp = places(cls, 0, c)
-        send(part.at[js(cls, c), :, zp, 1 - xh, yp], paired(cls, c), 4 + cls, qx.at[cls, c], along("x", 2))
+        send(part.at[js(cls, c), :, zp, 1 - xh, yp], paired(cls, c), 7 + 2 * cls + (c == 3), qx.at[cls, c], along("x", 2))
 
     def paired(cls, c):
-        return rx.at[cls, 3, js(cls, c)] if cls == 0 and c >= 3 else rx.at[cls, c]
+        return rx.at[cls, 3, pl.ds(0, 1)] if c == 3 else rx.at[cls, c]
 
     def pair_end(cls, c):
         if x_first(cls, c):
@@ -196,7 +216,7 @@
         return part.at[pl.ds(2 * cls, 2), i, zp, xh, yp]
 
     def late_send(cls, kind, c, i, step):
-        send(own_x(cls, i, c), r3.at[cls, kind], 7 + cls, q3.at[cls, min(kind, 2)], along(ring_axis[1 - cls], step))
+        send(own_x(cls, i, c), r3.at[cls, kind], 13 + cls, q3.at[cls, min(kind, 2)], along(ring_axis[1 - cls], step))
 
     def late0(cls):
         pair_end(cls, 0)
@@ -222,8 +242,6 @@
     def late3(cls):
         wait_bytes(r3.at[cls, pl.ds(2, 4)], q3.at[cls, 2])
         pair_end(cls, 3)
-        if cls == 0:
-            pair_end(cls, 4)
         first = own_x(cls, 0, 3)
         first[...] += r3[cls, 4] + r3[cls, 3]
         second = own_x(cls, 1, 3)
@@ -368,6 +386,7 @@
     m2_down(1, 1)
     product(2, 1, 2)
     ring_end(1, 0)
+    m1(1, 2)
     m3_up(0, 0)
     m3_down(0, 0)
     product(3, 0, 0)
@@ -375,8 +394,8 @@
     m3_down(1, 1)
     m2_up(0, 1)
     m2_down(0, 1)
+    second_pair()
     ladder_part(0)
-    m1(1, 2)
     ladder_part(1)
     m3_up(0, 1)
     m3_down(0, 1)
@@ -389,39 +408,46 @@
     m2_up(0, 2)
     m2_down(0, 2)
     ring_end(1, 1)
+    m3_up(1, 2)
+    m3_down(1, 2)
     first_pair_end()
     m1(1, 3)
+    m1(1, 4)
     late0(1)
-    m3_up(1, 2)
-    m3_down(1, 2)
     ring_end(0, 1)
     m3_up(0, 2)
     m3_down(0, 2)
     late0(0)
     m2_up(0, 3)
     m2_down(0, 3)
-    m2_up(0, 4)
-    m2_down(0, 4)
-    late1(1)
-    m3_up(0, 3)
-    m3_down(0, 3)
     ring_end(1, 2)
     m2_up(1, 3)
     m2_down(1, 3)
+    late1(1)
+    ladder_plane()
+    second_pair_end()
+    m3_up(0, 3)
+    m3_down(0, 3)
+    m2_up(0, 4)
+    m2_down(0, 4)
     m3_up(1, 3)
     m3_down(1, 3)
     m3_up(0, 4)
     m3_down(0, 4)
+    ring_end(0, 2)
     late1(0)
-    ring_end(0, 2)
-    ladder_plane()
+    m2_up(1, 4)
+    m2_down(1, 4)
+    m3_up(1, 4)
+    m3_down(1, 4)
     late2(1)
     late2(0)
     for name in ("itg", "his", "vir", "of", "os"):
         loads[name].wait()
+    ring_end(1, 3)
     ring_end(0, 3)
     ring_end(0, 4)
-    ring_end(1, 3)
+    ring_end(1, 4)
     rows = ladder_end()
     late3(1)
     sums = tail(1, rows, [jnp.zeros((8, 128), F32)] * 6)
@@ -480,7 +506,8 @@
             pltpu.VMEM((2, 2, 2, 4, 32, 256), F32),
             pltpu.VMEM((2, 6, 4, 2, 2, 32, 256), F32),
             pltpu.VMEM((2, 4, 2, 2, 32, 256), F32),
-            pltpu.VMEM((2, 2, 4, 32, 256), F32),
+            pltpu.VMEM((2, 4, 32, 256), F32),
+            pltpu.VMEM((3, 2, 32, 256), F32),
             pltpu.VMEM((2, 6, 2, 32, 256), F32),
             pltpu.VMEM((64, 4, 32, 256), bf16),
             pltpu.VMEM((4, 64, 256), F32),
@@ -497,13 +524,13 @@
             pltpu.VMEM((16, 1, 128), F32),
             pltpu.VMEM((8, 1, 128), F32),
             dma((17,)),
-            dma((9,)),
+            dma((15,)),
             dma((2,)),
-            dma((2, 4)),
+            dma((2, 5)),
             dma((2, 5)),
             dma((2, 5)),
             dma((2, 3)),
-            dma((1,)),
+            dma((2,)),
             dma((2,)), dma((2,)),
             dma((2,)), dma((2,)),
         ],

time: 65.2 us -> 65.1 us (level)
  no operation moved by 1% of the time
where the time goes in v4:
time: 65.1 us; the launch traced here: 65 us
  Pallas kernels  61.8 us (95%)
  between operations  1.81 us (3%)
  local copies, waits for them, and re-layouts  1.42 us (2%)
    pallas_call x1, Pallas kernels, shards(): pl.pallas_call(kernel, out_shape=(block, pltpu.VMEM((1, 128), F32)), in_s...  61.8 us
    squeeze x2, local copies, waits for them, and re-layouts, shards(): return (stacked[0], stacked[1], totals[0, :1], totals[0, 1:6])  1.42 us

profile of v4, /device:TPU:1, one launch (start us, length us, event | category | flops | bytes accessed | tf_op | source)
XLA Modules:
  0.0 65.0 jit_solution(3477690255666982478)
XLA Ops:
  0.6 61.8 %window.1 = (f32[2,2,4,32,256]{4,3,2,1,0:T(8,128)S(1)}, f32[1,128]{1,0:T(1,128)S(1)}) custom-call(f32[2,4,32,256]{3,2,1,0:T(8,128)} %amp_hbm.1, bf16[2,2048,256]{2,1,0:T(8,128)(2,1)} %bitcast.15, bf16[2048,4,1024]{2,1,0:T(4,128)(2,1)} %bitcast.14, bf16[64,4,32,256]{3,2,1,0:T(8,128)(2,1)} %lad_hbm.1, f32[2,4,32,256]{3,2,1,0:T(8,128)} %itg_hbm.1, ...), custom_call_target="tpu_custom_call" | custom-call | flops 8999999488 | bytes 27000000 | tf_op jit(solution)/shard_map/window/pallas_call | solution.py:496
  62.4 0.8 %slice_bitcast_fusion = (f32[2,4,32,256]{3,2,1,0:T(8,128)}, f32[2,4,32,256]{3,2,1,0:T(8,128)}) fusion(f32[2,2,4,32,256]{4,3,2,1,0:T(8,128)S(1)} %get-tuple-element.6), kind=kLoop, calls=%fused_computation | loop fusion | bytes 1048576 | tf_op jit(solution)/shard_map/squeeze | solution.py:553
  63.2 0.6 slice_bitcast_fusion.2

commit v5 on v4

--- a/solution.py
+++ b/solution.py
@@ -18,7 +18,7 @@
     both_ref, tot_ref,
     mbuf, ubuf, wbuf, part, r0, r1, rx, rf, rg, r3,
     lbuf, lgrp, lsum, lrecv_a, lplane, lrecv_b,
-    amp, itg, his, vir, of_ref, os_ref, sums_a, sums_b,
+    amp, itg, his, vir, of_ref, os_ref, sums_a,
     lsem, sent, q0, q1, qe, qx, q3, qf, sl, ql, ss, qs,
 ):
     wide = lax.axis_index("wide")
@@ -460,27 +460,26 @@
         one = jnp.sum(jnp.sum(s, axis=0, keepdims=True), axis=1, keepdims=True)
         mine = jnp.where(lane == n, one, mine)
 
-    def everyone(buf, own, row, devices, n):
-        count = len(devices)
-        buf[own] = row
-        for device in devices:
+    def totals():
+        me = wide * 4 + narrow
+        sums_a[me] = mine
+
+        def spread(d, carry):
+            peer = lax.rem(me + d, 128)
             pltpu.make_async_remote_copy(
-                src_ref=buf.at[own], dst_ref=buf.at[own], send_sem=ss.at[n], recv_sem=qs.at[n],
-                device_id=device, device_id_type=MESH,
+                src_ref=sums_a.at[me], dst_ref=sums_a.at[me], send_sem=ss.at[0], recv_sem=qs.at[0],
+                device_id={"wide": peer // 4, "narrow": lax.rem(peer, 4)}, device_id_type=MESH,
             ).start()
+            return carry
+
+        lax.fori_loop(1, 128, spread, 0)
+        others = sums_a.at[pl.ds(0, 127)]
         arrived = pltpu.make_async_remote_copy(
-            src_ref=buf.at[pl.ds(0, count)], dst_ref=buf.at[pl.ds(0, count)], send_sem=ss.at[n], recv_sem=qs.at[n],
-            device_id=devices[0], device_id_type=MESH,
+            src_ref=others, dst_ref=others, send_sem=ss.at[0], recv_sem=qs.at[0], device_id=plane[0], device_id_type=MESH
         )
         arrived.wait_recv()
-        return jnp.sum(buf[...], axis=0), arrived
-
-    def totals():
-        row, first = everyone(sums_a, z * 4 + y, mine, plane, 0)
-        row, second = everyone(sums_b, xpos * 2 + core, row, row_of_chips, 1)
-        tot_ref[...] = row * (1.0 / 8388608.0)
-        first.wait_send()
-        second.wait_send()
+        tot_ref[...] = jnp.sum(sums_a[...], axis=0) * (1.0 / 8388608.0)
+        arrived.wait_send()
 
     totals()
     arrivals(lrecv_a, 0).wait_send()
@@ -521,8 +520,7 @@
             pltpu.VMEM((1, 1024), F32),
             pltpu.VMEM((1, NI), F32),
             pltpu.VMEM((1, NJ), F32),
-            pltpu.VMEM((16, 1, 128), F32),
-            pltpu.VMEM((8, 1, 128), F32),
+            pltpu.VMEM((128, 1, 128), F32),
             dma((17,)),
             dma((15,)),
             dma((2,)),
@@ -532,7 +530,7 @@
             dma((2, 3)),
             dma((2,)),
             dma((2,)), dma((2,)),
-            dma((2,)), dma((2,)),
+            dma((1,)), dma((1,)),
         ],
         compiler_params=pltpu.CompilerParams(
             collective_id=0, has_side_effects=True, vmem_limit_bytes=52 * 2**20

time: 65.1 us -> 63.6 us (0.977)
  Pallas kernels: 61.8 us -> 60.3 us
    pallas_call x1, Pallas kernels: 61.8 us -> 60.3 us  [shards(): pl.pallas_call(kernel, out_shape=(block, pltpu.VMEM((1, 128), F32)), in_s...]
where the time goes in v5:
time: 63.6 us; the launch traced here: 63.5 us
  Pallas kernels  60.3 us (95%)
  between operations  1.81 us (3%)
  local copies, waits for them, and re-layouts  1.42 us (2%)
    pallas_call x1, Pallas kernels, shards(): pl.pallas_call(kernel, out_shape=(block, pltpu.VMEM((1, 128), F32)), in_s...  60.3 us
    squeeze x2, local copies, waits for them, and re-layouts, shards(): return (stacked[0], stacked[1], totals[0, :1], totals[0, 1:6])  1.42 us

profile of v5, /device:TPU:1, one launch (start us, length us, event | category | flops | bytes accessed | tf_op | source)
XLA Modules:
  0.0 63.5 jit_solution(10934236908606827282)
XLA Ops:
  0.6 60.3 %window.1 = (f32[2,2,4,32,256]{4,3,2,1,0:T(8,128)S(1)}, f32[1,128]{1,0:T(1,128)S(1)}) custom-call(f32[2,4,32,256]{3,2,1,0:T(8,128)} %amp_hbm.1, bf16[2,2048,256]{2,1,0:T(8,128)(2,1)} %bitcast.15, bf16[2048,4,1024]{2,1,0:T(4,128)(2,1)} %bitcast.14, bf16[64,4,32,256]{3,2,1,0:T(8,128)(2,1)} %lad_hbm.1, f32[2,4,32,256]{3,2,1,0:T(8,128)} %itg_hbm.1, ...), custom_call_target="tpu_custom_call" | custom-call | flops 8999999488 | bytes 27000000 | tf_op jit(solution)/shard_map/window/pallas_call | solution.py:495
  60.9 0.8 %slice_bitcast_fusion = (f32[2,4,32,256]{3,2,1,0:T(8,128)}, f32[2,4,32,256]{3,2,1,0:T(8,128)}) fusion(f32[2,2,4,32,256]{4,3,2,1,0:T(8,128)S(1)} %get-tuple-element.6), kind=kLoop, calls=%fused_computation | loop fusion | bytes 1048576 | tf_op jit(solution)/shard_map/squeeze | solution.py:551
  61.7 0.6 slice_bitcast_fusion.2
